TPU v7x, 32 devices: a whole 2x2x4 slice. The times are simulated.
32 devices in a mesh: dp: 16 (over z, y, core), tensor: 2 (over x).
Axes of the slice: x: 2, y: 2, z: 4, core: 2. Of those that a mesh axis runs over, the one named last changes fastest.
Arguments:
- tokens: bfloat16 [32, 1024, 768], P('dp', 'tensor'), may hold values from -6 to 6
- segment_ids: int32 [32, 1024], P('dp'), may hold values from 0 to 3, as said below
- timestep: int32 [32], P('dp'), may hold values from 0 to 999
- ln_gain: float32 [768], replicated, may hold values from 0.5 to 1.5
- query_key_value_weight: bfloat16 [3, 768, 768], P(None, None, 'tensor'), may hold values from -0.21875 to 0.21875
- output_projection: bfloat16 [768, 768], P('tensor'), may hold values from -1.75 to 1.75
- up_projection: bfloat16 [768, 3072], P(None, 'tensor'), may hold values from -0.21875 to 0.21875
- down_projection: bfloat16 [3072, 768], P('tensor'), may hold values from -0.109375 to 0.109375
- ada_weight: bfloat16 [128, 2304], replicated, may hold values from -0.5 to 0.5
- ada_bias: float32 [2304], replicated, may hold values from 0.5 to 1.5
- cotangent: bfloat16 [32, 1024, 768], P('dp', 'tensor')
Outputs:
- mixed: bfloat16 [32, 1024, 768], P('dp', 'tensor')
- d_tokens: bfloat16 [32, 1024, 768], P('dp', 'tensor')
- d_ln_gain: float32 [768], replicated
- d_qkv_weight: float32 [3, 768, 768], P(None, None, 'tensor')
- d_out_weight: float32 [768, 768], P('tensor')
- d_up_weight: float32 [768, 3072], P(None, 'tensor')
- d_down_weight: float32 [3072, 768], P('tensor')
- d_ada_weight: float32 [128, 2304], replicated
- d_ada_bias: float32 [2304], replicated
Inputs may be any that keep to these rules, and one draw needn't show every extreme that they name: `segment_ids`: within a sequence the ids never fall and start at 0; equal ids mark one document; the last token has id 3; one document of each sequence covers at least its positions 256 to 767.
All inputs are finite; a program needn't handle non-finite values.
Results may differ from a plain program's by a relative error of at most 0.02.
Values may be sent and summed in bfloat16 or wider, within the bound.
A program may use at most 320 MiB of HBM per device.

v0:
```python
import functools
import math

import jax
import jax.numpy as jnp
import numpy as np
from jax import lax
from jax.experimental import pallas as pl
from jax.experimental.pallas import tpu as pltpu
from jax.sharding import PartitionSpec as P

HD = 64
TEMB = 128
EPS = 1e-05
MASKED = -1000000000.0
f32 = jnp.float32
bf16 = jnp.bfloat16
VMEM_LIMIT = 62 * 1024 * 1024


def dot_nn(a, b):
    return lax.dot_general(a, b, (((1,), (0,)), ((), ())), preferred_element_type=f32)


def dot_nt(a, b):
    return lax.dot_general(a, b, (((1,), (1,)), ((), ())), preferred_element_type=f32)


def dot_tn(a, b):
    return lax.dot_general(a, b, (((0,), (0,)), ((), ())), preferred_element_type=f32)


def norm_parts(values):
    centred = values - jnp.mean(values, axis=-1, keepdims=True)
    variance = jnp.mean(centred * centred, axis=-1, keepdims=True)
    inverse = lax.rsqrt(variance + EPS)
    return centred * inverse, inverse


def norm_back(grad, normed, inverse):
    return inverse * (
        grad
        - jnp.mean(grad, axis=-1, keepdims=True)
        - normed * jnp.mean(grad * normed, axis=-1, keepdims=True)
    )


def rotary_np(length):
    half = HD // 2
    position = np.arange(length, dtype=np.float32)
    frequency = (10000.0 ** (-np.arange(half, dtype=np.float32) / half)).astype(np.float32)
    angles = position[:, None] * frequency[None, :]
    cosine, sine = np.cos(angles), np.sin(angles)
    cosine = np.concatenate([cosine, cosine] * 2, axis=1).astype(np.float32)
    sine = np.concatenate([-sine, sine] * 2, axis=1).astype(np.float32)
    return cosine, sine


def swap_halves(values):
    lane = lax.broadcasted_iota(jnp.int32, values.shape, 1)
    first = (lane % HD) < (HD // 2)
    return jnp.where(first, pltpu.roll(values, 128 - HD // 2, 1), pltpu.roll(values, HD // 2, 1))


def params(**kw):
    return pltpu.CompilerParams(vmem_limit_bytes=VMEM_LIMIT, **kw)


def cost(flops, nbytes, trans=0):
    return pl.CostEstimate(flops=int(flops), bytes_accessed=int(nbytes), transcendentals=int(trans))


BITS = {"core": 1, "y": 2, "zl": 4, "zh": 8}
MESH = pl.DeviceIdType.MESH


class Place:
    def __init__(self):
        self.me = lax.axis_index("dp")
        self.side = lax.axis_index("tensor")
        self.bit = {axis: (self.me // bit) % 2 for axis, bit in BITS.items()}
        self.partner = {
            axis: {"dp": self.me + bit * (1 - 2 * self.bit[axis])} for axis, bit in BITS.items()
        }
        self.partner["x"] = {"tensor": 1 - self.side}

    def greet(self, axes):
        barrier = pltpu.get_barrier_semaphore()
        for axis in axes:
            pl.semaphore_signal(barrier, inc=1, device_id=self.partner[axis], device_id_type=MESH)
        pl.semaphore_wait(barrier, len(axes))


ALL_AXES = ("core", "y", "zl", "zh", "x")


def remote(src, dst, send, recv, partner):
    return pltpu.make_async_remote_copy(
        src_ref=src, dst_ref=dst, send_sem=send, recv_sem=recv, device_id=partner, device_id_type=MESH
    )


class Reducer:
    STAGES = 5

    def __init__(self, place, view, rows, refs, order):
        self.place, self.view, self.order = place, view, order
        self.received, self.sends, self.recvs = refs[:5], refs[5], refs[6]
        self.cross = order.index("x")
        base, n = 0, rows
        self.spans = []
        for axis in order:
            if axis == "x":
                span = pl.ds(pl.multiple_of(base, 16), n)
                self.spans.append((span, span))
            else:
                n //= 2
                bit = place.bit[axis]
                keep = pl.ds(pl.multiple_of(base + bit * n, 16), n)
                send = pl.ds(pl.multiple_of(base + (1 - bit) * n, 16), n)
                self.spans.append((keep, send))
                base = base + bit * n

    @staticmethod
    def scratch(counts, rows, cols, order):
        shapes, n, cross = [], rows, False
        for slots, axis in zip(counts, order):
            if axis == "x":
                cross = True
            else:
                n //= 2
            shapes.append((slots, n, cols) if cross else (slots, 2, n, cols))
        return [pltpu.VMEM(shape, bf16) for shape in shapes] + [pltpu.SemaphoreType.DMA((sum(counts),))] * 2

    def slot(self, stage, c):
        return self.received[stage].at[c % self.received[stage].shape[0]]

    def flag(self, stage, c):
        before = sum(self.received[s].shape[0] for s in range(stage))
        return before + c % self.received[stage].shape[0]

    def copy(self, stage, c):
        send = self.spans[stage][1]
        if stage < self.cross:
            source = self.view(c).at[:, send, :]
        else:
            source = self.view(c).at[1 if stage == self.cross else 0, send, :]
        return remote(
            source,
            self.slot(stage, c),
            self.sends.at[self.flag(stage, c)],
            self.recvs.at[self.flag(stage, c)],
            self.place.partner[self.order[stage]],
        )

    def start(self, stage, c):
        self.copy(stage, c).start()

    def finish(self, stage, c, put=None):
        self.copy(stage, c).wait()
        keep = self.spans[stage][0]
        came, chunk = self.slot(stage, c), self.view(c)
        if stage < self.cross:
            for half in range(2):
                chunk[half, keep, :] += came[half]
        elif stage < 4:
            chunk[0, keep, :] += came[...]
        else:
            put(c, chunk[0, keep, :] + came[...])

    def step(self, stage, c, put=None):
        self.finish(stage, c, put)
        if stage + 1 < self.STAGES:
            self.start(stage + 1, c)


class Gatherer:
    STAGES = 4

    def __init__(self, place, view, rows, order, sends, recvs):
        self.place, self.view, self.sends, self.recvs = place, view, sends, recvs
        self.order = [axis for axis in order if axis != "x"][::-1]
        self.size = rows // 16
        bits = [place.bit[axis] for axis in self.order]
        self.bases = [sum(bits[j] * 2**j for j in range(stage, 4)) for stage in range(4)]

    def span(self, stage):
        n = self.size
        return self.view(pl.ds(pl.multiple_of(self.bases[stage] * n, 16), 2**stage * n))

    def copy(self, stage):
        span = self.span(stage)
        return remote(
            span, span, self.sends.at[stage], self.recvs.at[stage], self.place.partner[self.order[stage]]
        )

    def start(self, stage):
        self.copy(stage).start()

    def finish(self, stage):
        self.copy(stage).wait()


class Fetch:
    def __init__(self, place, own, other, rows, axes, sends, recvs):
        self.place, self.own, self.other, self.axes = place, own, other, axes
        self.sends, self.recvs = sends, recvs
        self.size = rows // 2 ** len(axes)
        bits = [place.bit[axis] for axis in axes]
        self.bases = [sum(bits[j] * 2**j for j in range(s, len(axes))) for s in range(len(axes))]

    def copy(self, stage):
        level = max(stage - 1, 0)
        n = self.size
        span = pl.ds(pl.multiple_of(self.bases[level] * n, 16), 2**level * n)
        source = self.own(span) if stage == 0 else self.other(span)
        axis = "x" if stage == 0 else self.axes[stage - 1]
        return remote(
            source, self.other(span), self.sends.at[stage], self.recvs.at[stage], self.place.partner[axis]
        )

    def start(self, stage):
        self.copy(stage).start()

    def step(self, stage):
        self.copy(stage).wait()
        if stage < len(self.axes):
            self.copy(stage + 1).start()


def qkv_rows(row, rows, x_ref, gain_ref, w_ref, cos_ref, sin_ref, n_ref, q_ref, k_ref, v_ref, first):
    span = pl.ds(row, rows)
    pairs = w_ref.shape[2] // 128
    if n_ref is None:
        normed = x_ref[span, :]
    else:
        normed, _ = norm_parts(x_ref[span, :].astype(f32))
        normed = (normed * gain_ref[...].reshape(1, -1)).astype(bf16)
        n_ref[span, :] = normed
    cosine, sine = cos_ref[span, :], sin_ref[span, :]
    for which, out in ((0, q_ref), (1, k_ref)):
        raw = dot_nn(normed, w_ref[which])
        for pair in range(pairs):
            part = raw[:, pair * 128 : pair * 128 + 128]
            turned = (part * cosine + swap_halves(part) * sine).astype(bf16)
            if which == 0:
                turned = turned * jnp.asarray(0.125, bf16)
            out[first + pair, span, :] = turned
    raw = dot_nn(normed, w_ref[2]).astype(bf16)
    for pair in range(pairs):
        v_ref[first + pair, span, :] = raw[:, pair * 128 : pair * 128 + 128]


EDGE = 256


def mask_scores(scores, inner, column, segr):
    length = scores.shape[1]
    last = length - EDGE
    middle = segr[:, length // 2 : length // 2 + 128]
    if inner:
        bias = jnp.where(jnp.concatenate([middle] * (length // 128), axis=1) == segr, 0.0, MASKED)
        parts = [scores[:, :EDGE] + bias[:, :EDGE], scores[:, EDGE:last], scores[:, last:] + bias[:, last:]]
    else:
        wide = jnp.concatenate([column] * (EDGE // 128), axis=1)
        inside = column == middle
        parts = (
            [jnp.where(wide == segr[:, :EDGE], scores[:, :EDGE], MASKED)]
            + [jnp.where(inside, scores[:, j : j + 128], MASKED) for j in range(EDGE, last, 128)]
            + [jnp.where(wide == segr[:, last:], scores[:, last:], MASKED)]
        )
    return jnp.concatenate(parts, axis=1)


def attend_rows(pair, spans, q_ref, k_ref, v_ref, segc_ref, segr, o_ref, lse_ref):
    lane = lax.broadcasted_iota(jnp.int32, (1, 128), 1)
    low = lane < HD
    mine = (low, jnp.logical_not(low))
    k, v = k_ref[pair], v_ref[pair]
    one = jnp.ones_like(v)
    values = [jnp.where(m, v, one) for m in mine]
    units = [(span, inner, head) for span, inner in spans for head in range(2)]

    def score(unit):
        span, _, head = unit
        q = q_ref[pair, span, :]
        return dot_nt(jnp.where(mine[head], q, jnp.zeros_like(q)), k)

    ahead = 2
    scores = [score(unit) for unit in units[:ahead]]
    parts = []
    for i, (span, inner, head) in enumerate(units):
        if i + ahead < len(units):
            scores.append(score(units[i + ahead]))
        masked = mask_scores(scores[i], inner, segc_ref[span, :], segr)
        largest = jnp.max(masked, axis=1, keepdims=True)
        weights = jnp.exp(masked - largest).astype(bf16)
        mixed = dot_nn(weights, values[head])
        total = pltpu.roll(mixed, HD, 1)
        parts.append((mixed / total, largest + jnp.log(total)))
        if head == 1:
            (out0, lse0), (out1, lse1) = parts[-2:]
            o_ref[span, pl.ds(pl.multiple_of(pair * 128, 128), 128)] = jnp.where(low, out0, out1).astype(bf16)
            lse = jnp.where(low, lse0, lse1).T
            lse_ref[pair, 0:1, span] = lse[0:1, :]
            lse_ref[pair, 1:2, span] = lse[HD : HD + 1, :]


def gelu_both(u):
    c0 = math.sqrt(2.0 / math.pi)
    square = u * u
    t = jnp.tanh(u * (c0 + (c0 * 0.044715) * square))
    half = 0.5 + 0.5 * t
    act = u * half
    slope = half + (0.5 * u) * (1.0 - t * t) * (c0 + (3.0 * c0 * 0.044715) * square)
    return act, slope


FEED_STEPS = 6
UP_ORDER = ("core", "y", "zl", "x", "zh")
DOWN_ORDER = ("core", "x", "zl", "y", "zh")
QKV_ORDERS = (
    ("core", "y", "x", "zl", "zh"),
    ("core", "x", "y", "zl", "zh"),
    ("core", "zl", "x", "y", "zh"),
)


def attend_back(
    pair, q_ref, k_ref, v_ref, o_ref, do_ref, lse_ref, segc_ref, segr, cos_ref, sin_ref, acc_ref, poll
):
    length = o_ref.shape[0]
    rows = 256
    lane = lax.broadcasted_iota(jnp.int32, (1, 128), 1)
    low = lane < HD
    lanes = pl.ds(pl.multiple_of(pair * 128, 128), 128)
    q, do = q_ref[pair], do_ref[:, lanes]
    product = do.astype(f32) * o_ref[:, lanes].astype(f32)
    high_part = product.astype(bf16)
    low_part = (product - high_part.astype(f32)).astype(bf16)
    row8 = lax.broadcasted_iota(jnp.int32, (8, 128), 0)
    lane8 = lax.broadcasted_iota(jnp.int32, (8, 128), 1)
    select = jnp.where((lane8 // HD) == row8, 1.0, 0.0).astype(bf16)
    delta = dot_nt(select, high_part) + dot_nt(select, low_part)
    lse = lse_ref[pair]
    zero = jnp.zeros_like(q)
    q_heads = (jnp.where(low, q, zero), jnp.where(low, zero, q))
    do_heads = (jnp.where(low, do, zero), jnp.where(low, zero, do))
    acc_ref[...] = jnp.zeros_like(acc_ref)
    mine = (low, jnp.logical_not(low))
    blocks = length // rows
    for group in range(2):
        if group == 1:
            poll()
        units = [(block, head) for block in (3 * group, 1 + group) for head in range(2)]

        def products(unit):
            block, head = unit
            span = pl.ds(block * rows, rows)
            k, v = k_ref[pair, span, :], v_ref[pair, span, :]
            kh = jnp.where(mine[head], k, jnp.zeros_like(k))
            vh = jnp.where(mine[head], v, jnp.zeros_like(v))
            return kh, dot_nt(kh, q), dot_nt(vh, do)

        ahead = 1
        ready = [products(unit) for unit in units[:ahead]]
        dq = jnp.zeros((128, length), f32)
        for i, (block, head) in enumerate(units):
            if i + ahead < len(units):
                ready.append(products(units[i + ahead]))
            kh, scores, d_probs = ready[i]
            span = pl.ds(block * rows, rows)
            inner = block * rows >= EDGE and (block + 1) * rows <= length - EDGE
            scores = mask_scores(scores, inner, segc_ref[span, :], segr)
            probs = jnp.exp(scores - lse[head : head + 1, :])
            part_v = dot_nn(probs.astype(bf16), do_heads[head])
            d_scores = (probs * (d_probs - delta[head : head + 1, :])).astype(bf16)
            part_k = dot_nn(d_scores, q_heads[head])
            dq = dq + dot_tn(kh, d_scores)
            if head == 0:
                dv, dk = part_v, part_k
            else:
                dv, dk = dv + part_v, dk + part_k
                cosine, sine = cos_ref[span, :], sin_ref[span, :]
                k_ref[pair, span, :] = (dk * cosine - swap_halves(dk) * sine).astype(bf16)
                v_ref[pair, span, :] = dv.astype(bf16)
        acc_ref[...] += dq
    dq = acc_ref[...].T * 0.125
    q_ref[pair] = (dq * cos_ref[...] - swap_halves(dq) * sin_ref[...]).astype(bf16)


SPREAD_ORDER = ("zh", "zl", "y", "x", "core")


def layer_kernel(
    tok, cot_in, wq, wo, wu, wd, gain_ref, seg_ref, cos_ref, sin_ref, emb_ref, ada_ref, bias_ref,
    oq, oo, ou, od, up_out, down_out, out_out, qkv_out, mixed_out, dtok_out, dada_out, dbias_ref, dgain_ref,
    xs, ns, qs, ks, vs, os, ls, segc, wqs, wos, cot, mod,
    hidden, modul, modul_t, dbranch, branch, dmod, acts, dups, upbuf, downbuf, acc,
    ups, downs, fin_up, fin_down, fin_out, fin_qkv, every, gains, gains_in,
    local, xsend, xrecv, wsend, wrecv, loads,
    fsend, frecv, asend, arecv, gsend, grecv, ssend, srecv, *reducing,
):
    place = Place()
    side = place.side
    length, width = xs.shape
    half = length // 2
    rows = 256
    blocks = length // rows
    block = wu.shape[1] // FEED_STEPS
    heads = wo.shape[0]
    hid = wu.shape[1]
    tiles = 3 * width // 128
    own_rows = pl.ds(pl.multiple_of(side * half, half), half)
    other_rows = pl.ds(pl.multiple_of((1 - side) * half, half), half)

    def copy_here(src, dst, index):
        copy = pltpu.make_async_copy(src, dst, local.at[index])
        copy.start()
        return copy

    place.greet(ALL_AXES)
    send_tok = remote(tok.at[1 - side], xs.at[own_rows, :], xsend.at[0], xrecv.at[0], place.partner["x"])
    send_cot = remote(cot_in.at[1 - side], cot.at[own_rows, :], xsend.at[1], xrecv.at[1], place.partner["x"])

    def up_view(g):
        return lambda r, s: r.at[s, pl.ds(g * hid // 3, hid // 3)]

    def down_view(g):
        return lambda r, s: r.at[pl.ds(g * hid // 3, hid // 3)].at[s, :]

    plan = (
        (lambda r, s: r.at[2, s, :], wq, oq, width, ("y", "zl", "core")),
        (lambda r, s: r.at[0, s, :], wq, oq, width, ("y", "core")),
        (lambda r, s: r.at[1, s, :], wq, oq, width, ("zl", "core")),
        (lambda r, s: r.at[s, :], wo, oo, heads, ("y", "zl", "core")),
        (up_view(0), wu, ou, width, ("y", "zl", "core")),
        (down_view(0), wd, od, hid // 3, ("zl", "y", "core")),
        (up_view(1), wu, ou, width, ("y", "zl", "core")),
        (down_view(1), wd, od, hid // 3, ("zl", "y", "core")),
        (up_view(2), wu, ou, width, ("y", "zl", "core")),
        (down_view(2), wd, od, hid // 3, ("zl", "y", "core")),
    )
    V, Q, K, OUT, UP0, DN0, UP1, DN1, UP2, DN2 = range(10)
    fetches = [
        Fetch(place, functools.partial(view, own), functools.partial(view, other), n, axes, wsend.at[i], wrecv.at[i])
        for i, (view, own, other, n, axes) in enumerate(plan)
    ]
    send_tok.start()
    for index in (V, Q, K, OUT, UP0, DN0, UP1, DN1):
        fetches[index].start(0)
    send_cot.start()
    for index in (UP2, DN2):
        fetches[index].start(0)

    get_x = copy_here(tok.at[side], xs.at[own_rows, :], 0)
    get_w = copy_here(wq, wqs.at[0], 1)
    get_cot = copy_here(cot_in.at[side], cot.at[own_rows, :], 2)
    get_wo = copy_here(wo, wos.at[pl.ds(0, heads), :], 3)

    segr = seg_ref[pl.ds(side, 1), :].astype(f32)
    segc[...] = jnp.broadcast_to(segr, (128, length)).T
    emb = jnp.broadcast_to(emb_ref[pl.ds(side, 1), :], (TEMB, TEMB)).T
    for tile in range(tiles):
        span = slice(tile * 128, tile * 128 + 128)
        value = jnp.sum(emb * ada_ref[:, span].astype(f32), axis=0, keepdims=True) + bias_ref[span].reshape(1, -1)
        start = tile * 128 % width
        mod[tile * 128 // width : tile * 128 // width + 1, start : start + 128] = value
    get_x.wait()
    get_w.wait()

    def qkv_half(base, w_ref, w_first, n_ref):
        def step(i, carry):
            row = pl.multiple_of(base + i * rows, rows)
            qkv_rows(
                row, rows, xs if n_ref is not None else ns, gain_ref, w_ref, cos_ref, sin_ref,
                n_ref, qs, ks, vs, w_first,
            )
            return carry

        lax.fori_loop(0, half // rows, step, 0)

    qkv_half(side * half, wqs.at[0], 0, ns)
    send_tok.wait()
    qkv_half((1 - side) * half, wqs.at[0], 0, ns)

    per_pair = 2
    steps = 6 * per_pair
    events = {
        0: ((V, 0),),
        2: ((V, 1), (Q, 0)),
        3: ((K, 0),),
        4: ((OUT, 0),),
        5: ((V, 2), (Q, 1), (UP0, 0)),
        6: ((OUT, 1), (UP0, 1), (DN0, 1)),
        7: ((UP1, 0), (DN1, 0)),
        10: ((DN0, 2), (OUT, 2)),
        11: ((UP0, 2), (UP1, 1)),
    }

    def attend(step, carry):
        pair = step // per_pair

        @pl.when(step == steps // 2)
        def _():
            fetches[K].step(1)
            fetches[DN0].step(0)
            for index in (V, Q, K):
                fetches[index].step(len(fetches[index].axes))
            copy = copy_here(oq, wqs.at[1], 1)
            copy.wait()
            qkv_half(0, wqs.at[1], 3, None)
            qkv_half(half, wqs.at[1], 3, None)

        for at, moves in events.items():

            @pl.when(step == at)
            def _(moves=moves):
                for index, stage in moves:
                    fetches[index].step(stage)

        part = step % per_pair
        edge = pl.ds(pl.multiple_of(part * (length - rows), rows), rows)
        inner = pl.ds(pl.multiple_of((1 + part) * rows, rows), rows)
        attend_rows(pair, ((edge, False), (inner, True)), qs, ks, vs, segc, segr, os, ls)
        return carry

    lax.fori_loop(0, steps, attend, 0)

    def load_weights(step):
        slot = step % 2
        span = pl.ds(pl.multiple_of(step * block, 128), block)
        return [
            pltpu.make_async_copy(wu.at[:, span], upbuf.at[slot, :, pl.ds(0, block)], loads.at[slot, 0]),
            pltpu.make_async_copy(ou.at[:, span], upbuf.at[slot, :, pl.ds(block, block)], loads.at[slot, 1]),
            pltpu.make_async_copy(wd.at[span, :], downbuf.at[slot, pl.ds(0, block), :], loads.at[slot, 2]),
            pltpu.make_async_copy(od.at[span, :], downbuf.at[slot, pl.ds(block, block), :], loads.at[slot, 3]),
        ]

    fetches[OUT].step(3)
    get_wo.wait()
    copy_here(oo, wos.at[pl.ds(heads, heads), :], 3).wait()
    get_cot.wait()
    fetches[DN1].step(1)
    fetches[UP0].step(3)
    fetches[DN0].step(3)
    for copy in load_weights(0):
        copy.start()

    def middle(i, carry):
        span = pl.ds(pl.multiple_of(i * rows, rows), rows)
        shift, scale = mod[0:1, :], mod[1:2, :]
        h = xs[span, :].astype(f32) + dot_nn(os[span, :], wos[...])
        hidden[span, :] = h
        normed, _ = norm_parts(h)
        m = (normed * (1.0 + scale) + shift).astype(bf16)
        modul[span, :] = m
        modul_t[:, span] = m.T
        branch[span, :] = jnp.zeros((rows, width), f32)
        dmod[span, :] = jnp.zeros((rows, width), f32)
        return carry

    lax.fori_loop(0, blocks, middle, 0)

    def to_branch(part):
        span = own_rows if part == 0 else other_rows
        dbranch[span, :] = (cot[span, :].astype(f32) * mod[2:3, :]).astype(bf16)

    to_branch(0)
    send_cot.wait()
    to_branch(1)

    def track(c, t):
        if isinstance(c, int) and c == 0:
            return upbuf.at[:, :, pl.ds(t * 128, 128)]
        index = 3 * (c - 1) + t
        return ups.at[index // 2, :, :, pl.ds(pl.multiple_of((index % 2) * 128, 128), 128)]

    feeders = [
        Reducer(place, lambda c: ups.at[c], width, reducing[0:7], UP_ORDER),
        Reducer(place, lambda c: downs.at[c], block, reducing[7:14], DOWN_ORDER),
    ]
    movers = [
        Reducer(
            place, functools.partial(track, t=t), width, reducing[14 + 7 * t : 21 + 7 * t], QKV_ORDERS[t]
        )
        for t in range(3)
    ]

    def put_up(c, value):
        fin_up[:, pl.ds(pl.multiple_of(c * block, 128), block)] = value

    def put_down(c, value):
        fin_down[c] = value

    def feed_event(stage, c):
        for reducer, put in zip(feeders, (put_up, put_down)):
            reducer.step(stage, c, put)

    def put_final(t):
        def put(c, value):
            if c == 0:
                fin_out[t] = value
            else:
                fin_qkv[c - 1, t] = value

        return put

    def move_event(stage, c):
        for t, reducer in enumerate(movers):
            reducer.step(stage, c, put_final(t))

    FIRST = (3, 6, 9)
    LATER = {
        0: {3: 12, 4: 15},
        1: {3: 14, 4: 17},
        2: {2: 13, 3: 16, 4: 18},
        3: {1: 12, 2: 16, 3: 18, 4: 20},
        4: {1: 14, 2: 18, 3: 20, 4: 22},
        5: {0: 13, 1: 18, 2: 20, 3: 22, 4: 23},
    }

    def feed_polls(t, stages):
        for stage in stages:
            since = t - FIRST[stage]

            @pl.when(since >= 0)
            def _(stage=stage, c=since // 2):
                feed_event(stage, c)

    def feed(step, carry):
        feed_polls(2 * step, (1,))
        @pl.when(step == 1)
        def _():
            fetches[UP1].step(3)
            fetches[DN1].step(3)

        @pl.when(step == 3)
        def _():
            fetches[UP2].step(2)
            fetches[DN2].step(2)

        for copy in load_weights(step):
            copy.wait()

        slot = step % 2
        up, down = upbuf.at[slot], downbuf.at[slot]
        for i in range(blocks):
            span = pl.ds(i * rows, rows)
            u = dot_nn(modul[span, :], up[...])
            act, slope = gelu_both(u)
            act = act.astype(bf16)
            acts[span, :] = act
            d_act = dot_nt(dbranch[span, :], down[...])
            d_up = (d_act * slope).astype(bf16)
            dups[span, :] = d_up
            branch[span, :] += dot_nn(act, down[...])
            dmod[span, :] += dot_nt(d_up, up[...])
        feed_polls(2 * step + 1, (2, 0))

        @pl.when(step == 0)
        def _():
            fetches[UP1].step(2)
            fetches[DN1].step(2)
            fetches[UP2].step(0)
            fetches[DN2].step(0)

        @pl.when(step == 1)
        def _():
            fetches[UP2].step(1)
            fetches[DN2].step(1)

        @pl.when(step == 3)
        def _():
            fetches[UP2].step(3)
            fetches[DN2].step(3)

        @pl.when(step + 1 < FEED_STEPS)
        def _():
            for copy in load_weights(step + 1):
                copy.start()

        grad = dot_nn(modul_t[...], dups[...]).astype(bf16)
        ups[step, 0] = grad[:, :block]
        ups[step, 1] = grad[:, block:]
        feeders[0].start(0, step)
        grad = dot_tn(acts[...], dbranch[...]).astype(bf16)
        downs[step, 0] = grad[:block]
        downs[step, 1] = grad[block:]
        feeders[1].start(0, step)
        return carry

    lax.fori_loop(0, FEED_STEPS, feed, 0)

    feed_schedule = {}
    for c, ends in LATER.items():
        for stage, t in ends.items():
            feed_schedule.setdefault(t, []).append((stage, c))

    def feed_static(t):
        for stage, c in feed_schedule.get(t, []):
            feed_event(stage, c)

    sums = dgain_ref
    sums[...] = jnp.zeros_like(sums)
    def between(i, carry):
        for k in range(blocks):

            @pl.when(i == k)
            def _(k=k):
                feed_static(2 * FEED_STEPS + k)

        span = pl.ds(pl.multiple_of(i * rows, rows), rows)
        scale, gate = mod[1:2, :], mod[2:3, :]
        h = hidden[span, :]
        dout = cot[span, :].astype(f32)
        br = branch[span, :]
        cot[span, :] = (h + gate * br).astype(bf16)
        normed, inverse = norm_parts(h)
        dm = dmod[span, :]
        sums[0:1, :] += jnp.sum(dm, axis=0, keepdims=True)
        sums[1:2, :] += jnp.sum(dm * normed, axis=0, keepdims=True)
        sums[2:3, :] += jnp.sum(dout * br, axis=0, keepdims=True)
        dh = dout + norm_back(dm * (1.0 + scale), normed, inverse)
        hidden[span, :] = dh
        dattn = dh.astype(bf16)
        modul[span, :] = dattn
        dbranch[span, :] = dot_nt(dattn, wos[...]).astype(bf16)
        return carry

    lax.fori_loop(0, blocks, between, 0)
    grad = dot_tn(os[...], modul[...]).astype(bf16)
    for t in range(3):
        chunk = track(0, t)
        for i in range(2):
            part = grad[i * heads : (i + 1) * heads]
            chunk[i, :heads, :] = part[:, t * 128 : t * 128 + 128]
            chunk[i, heads:, :] = part[:, heads + t * 128 : heads + t * 128 + 128]
        movers[t].start(0, 0)
    feed_static(16)

    number = sum(
        (side if axis == "x" else place.bit[axis]) * 2**i for i, axis in enumerate(SPREAD_ORDER)
    )
    every[pl.ds(number, 1)] = jnp.zeros((1,) + every.shape[1:], f32)
    for tile in range(tiles):
        line, lane = tile * 128 // width, tile * 128 % width
        every[pl.ds(number, 1), tile : tile + 1, :] = sums[line : line + 1, lane : lane + 128][None]
    every[pl.ds(number, 1), tiles : tiles + 1, :] = emb_ref[pl.ds(side, 1), :][None]

    def spread(stage):
        span = every.at[pl.ds(number - number % 2**stage, 2**stage)]
        return remote(span, span, ssend.at[stage], srecv.at[stage], place.partner[SPREAD_ORDER[stage]])

    spread(0).start()

    def send_mixed(i):
        n = half // 4
        span = pl.ds(pl.multiple_of((1 - side) * half + i * n, n), n)
        return remote(
            cot.at[span, :], mixed_out.at[side, pl.ds(i * n, n), :],
            xsend.at[2 + i], xrecv.at[2 + i], place.partner["x"],
        )

    keep_mixed = copy_here(cot.at[own_rows, :], mixed_out.at[side], 4)
    modul_t[...] = ns[...].T

    def gather_ffn(g):
        cols = hid // 2
        return [
            Gatherer(
                place, lambda s: up_out.at[s, pl.ds(g * cols, cols)], width, UP_ORDER, fsend.at[g, 0], frecv.at[g, 0]
            ),
            Gatherer(
                place, lambda s: down_out.at[pl.ds(3 * g, 3), s, :], block, DOWN_ORDER, fsend.at[g, 1], frecv.at[g, 1]
            ),
        ]

    def gather_qkv(t, first, count):
        lanes = pl.ds((first - 1) * 128, count * 128)
        return Gatherer(
            place, lambda s: qkv_out.at[t, s, lanes], width, QKV_ORDERS[t],
            asend.at[first - 1, t], arecv.at[first - 1, t],
        )

    def gather_out(t):
        lanes = pl.ds(t * 128, 128)
        return Gatherer(
            place, lambda s: out_out.at[s, lanes], width, QKV_ORDERS[t], asend.at[1, t], arecv.at[1, t]
        )

    def put_pieces(gathers, sources):
        copies = [
            pltpu.make_async_copy(source, gather.span(0), local.at[8 + i])
            for i, (gather, source) in enumerate(zip(gathers, sources))
        ]
        for copy in copies:
            copy.start()
        for copy in copies:
            copy.wait()

    def gather_event(gathers, stage):
        for gather in gathers:
            if stage >= 0:
                gather.finish(stage)
            if stage + 1 < Gatherer.STAGES:
                gather.start(stage + 1)

    ffn = [gather_ffn(0), gather_ffn(1)]

    def start_ffn(g):
        cols = hid // 2
        put_pieces(ffn[g], [fin_up.at[:, pl.ds(g * cols, cols)], fin_down.at[pl.ds(3 * g, 3)]])
        gather_event(ffn[g], -1)

    outs = [gather_out(t) for t in range(3)]
    gathers = {c: [gather_qkv(t, c, 1) for t in range(3)] for c in (1, 2, 3)}

    def start_qkv(c):
        put_pieces(gathers[c], [fin_qkv.at[c - 1, t] for t in range(3)])
        gather_event(gathers[c], -1)

    def start_out():
        put_pieces(outs, [fin_out.at[t] for t in range(3)])
        gather_event(outs, -1)

    back_events = {}

    def at(t, event, *operands):
        back_events.setdefault(t, []).append(functools.partial(event, *operands))

    for t, moves in feed_schedule.items():
        for stage, c in moves:
            if t > 16:
                at(t, feed_event, stage, c)
    for c, times in ((0, (17, 20, 21, 22, 24)), (1, (22, 24, 25, 26, 28)), (2, (26, 28))):
        for stage, t in enumerate(times):
            at(t, move_event, stage, c)
    at(19, start_ffn, 0)
    for stage, t in enumerate((22, 25, 27, 28)):
        at(t, gather_event, ffn[0], stage)
    at(23, start_ffn, 1)
    for stage, t in enumerate((26, 28)):
        at(t, gather_event, ffn[1], stage)
    at(24, start_out)
    for stage, t in enumerate((26, 28)):
        at(t, gather_event, outs, stage)
    at(28, lambda: start_qkv(1))

    def spread_event(stage):
        spread(stage).wait()
        if stage < 4:
            spread(stage + 1).start()

    for stage in range(5):
        at(18 + 2 * stage, spread_event, stage)
    for i in range(4):
        at(18 + 2 * i, lambda i: send_mixed(i).start(), i)

    def back_polls(step, which):
        for t, moves in back_events.items():
            if t >= 17 and (t - 17) % 2 == which:

                @pl.when(step == (t - 17) // 2)
                def _(moves=moves):
                    for move in moves:
                        move()

    def back(step, carry):
        pair = step // 2 + 3 * (step % 2)
        back_polls(step, 0)
        attend_back(
            pair, qs, ks, vs, os, dbranch, ls, segc, segr, cos_ref, sin_ref, acc,
            lambda: back_polls(step, 1),
        )
        for t, ref in enumerate((qs, ks, vs)):
            grad = dot_nn(modul_t[...], ref[pair]).astype(bf16)
            track(1 + step // 2, t)[step % 2] = grad

        @pl.when(step % 2 == 1)
        def _():
            for reducer in movers:
                reducer.start(0, 1 + step // 2)

        return carry

    lax.fori_loop(0, 6, back, 0)

    def gain_copy(stage):
        return remote(
            gains.at[stage], gains_in.at[stage], gsend.at[stage], grecv.at[stage],
            place.partner[ALL_AXES[stage]],
        )

    send_dtok = remote(modul.at[other_rows, :], dtok_out.at[side], xsend.at[6], xrecv.at[6], place.partner["x"])
    def gain_event(stage):
        gain_copy(stage).wait()
        total = gains[stage] + gains_in[stage]
        if stage < 4:
            gains[stage + 1] = total
            gain_copy(stage + 1).start()
        else:
            dgain_ref[...] = total

    def last_rows(i):
        b = ((1 - side) * (blocks // 2) + i) % blocks
        span = pl.ds(pl.multiple_of(b * rows, rows), rows)
        dnormed = jnp.zeros((rows, width), f32)
        for which, ref in enumerate((qs, ks, vs)):
            for group in range(2):
                grad = jnp.concatenate([ref[3 * group + p, span, :] for p in range(3)], axis=1)
                dnormed = dnormed + dot_nt(grad, wqs[group, which])
        normed, inverse = norm_parts(xs[span, :].astype(f32))
        gains[0, 0:1, :] += jnp.sum(dnormed * normed, axis=0, keepdims=True)
        modul[span, :] = (
            hidden[span, :] + norm_back(dnormed * gain_ref[...].reshape(1, -1), normed, inverse)
        ).astype(bf16)

    gains[0] = jnp.zeros(gains.shape[1:], f32)
    move_event(2, 2)
    gather_event(outs, 2)
    move_event(0, 3)

    def after_rows(i):
        if i == 0:
            move_event(3, 2)
            gather_event(gathers[1], 0)
            gather_event(ffn[1], 2)
        elif i == 1:
            gather_event(outs, 3)
            move_event(1, 3)
            send_dtok.start()
            move_event(4, 2)
            start_qkv(2)
            gather_event(ffn[1], 3)
        elif i == 2:
            gather_event(gathers[1], 1)

    def last_step(i, carry):
        last_rows(i)
        for k in range(blocks - 1):

            @pl.when(i == k)
            def _(k=k):
                after_rows(k)

        return carry

    lax.fori_loop(0, blocks, last_step, 0)
    move_event(2, 3)
    gather_event(gathers[2], 0)
    gain_copy(0).start()
    keep_dtok = copy_here(modul.at[own_rows, :], dtok_out.at[side], 5)
    gather_event(gathers[1], 2)
    embeddings = every[:, tiles, :]
    for tile in range(tiles):
        part = every[:, tile, :]
        lane = slice(tile * 128, tile * 128 + 128)
        line, start = tile * 128 // width, tile * 128 % width
        branch[line * TEMB : (line + 1) * TEMB, start : start + 128] = lax.dot_general(
            embeddings, part, (((0,), (0,)), ((), ())),
            preferred_element_type=f32, precision=lax.Precision.HIGHEST,
        )
        dbias_ref[0:1, lane] = jnp.sum(part, axis=0, keepdims=True)
    put_dada = copy_here(branch.at[pl.ds(0, 3 * TEMB), :], dada_out, 6)
    move_event(3, 3)
    gain_event(0)
    gather_event(gathers[2], 1)
    gather_event(gathers[1], 3)
    move_event(4, 3)
    start_qkv(3)
    gain_event(1)
    gather_event(gathers[2], 2)
    gather_event(gathers[3], 0)
    gain_event(2)
    gather_event(gathers[2], 3)
    gather_event(gathers[3], 1)
    gain_event(3)
    gather_event(gathers[3], 2)
    gather_event(gathers[3], 3)
    gain_event(4)
    for i in range(4):
        send_mixed(i).wait()
    keep_mixed.wait()
    send_dtok.wait()
    keep_dtok.wait()
    put_dada.wait()


def layer_call(tokens, cot, wq, wo, wu, wd, gain, segments, cosine, sine, embedding, ada, bias):
    length, width = 2 * tokens.shape[1], tokens.shape[2]
    half, hid = wq.shape[2], wu.shape[1]
    block = hid // FEED_STEPS
    pairs = width // 128
    any_ = pl.BlockSpec(memory_space=pl.ANY)
    vm = pl.BlockSpec(memory_space=pltpu.VMEM)
    shape = jax.ShapeDtypeStruct
    dma = pltpu.SemaphoreType.DMA
    low = lambda *dims: pltpu.VMEM(dims, bf16)
    full = lambda *dims: pltpu.VMEM(dims, f32)
    slots = (2, 4, 4, 4, 4)
    reducing = Reducer.scratch(slots, width, block, UP_ORDER)
    reducing += Reducer.scratch(slots, block, width, DOWN_ORDER)
    for order in QKV_ORDERS:
        reducing += Reducer.scratch((2,) * 5, width, 128, order)
    return pl.pallas_call(
        layer_kernel,
        in_specs=[any_] * 6 + [vm] * 7,
        out_specs=[any_] * 11 + [vm] * 2,
        out_shape=[
            shape(wq.shape, bf16),
            shape(wo.shape, bf16),
            shape(wu.shape, bf16),
            shape(wd.shape, bf16),
            shape((width, hid), bf16),
            shape((FEED_STEPS, block, width), bf16),
            shape((width, half), bf16),
            shape(wq.shape, bf16),
            shape((2, length // 2, width), bf16),
            shape((2, length // 2, width), bf16),
            shape((3 * TEMB, width), f32),
            shape((8, 3 * width), f32),
            shape((8, width), f32),
        ],
        scratch_shapes=[
            low(length, width),
            low(length, width),
            low(pairs, length, 128),
            low(pairs, length, 128),
            low(pairs, length, 128),
            low(length, width),
            full(pairs, 8, length),
            full(length, 128),
            low(2, *wq.shape),
            low(width, width),
            low(length, width),
            full(8, width),
            full(length, width),
            low(length, width),
            low(width, length),
            low(length, width),
            full(length, width),
            full(length, width),
            low(length, 2 * block),
            low(length, 2 * block),
            low(2, width, 2 * block),
            low(2, 2 * block, width),
            full(128, length),
            low(FEED_STEPS, 2, width, block),
            low(FEED_STEPS, 2, block, width),
            low(width // 16, hid),
            low(FEED_STEPS, block // 16, width),
            low(3, width // 16, 128),
            low(3, 3, width // 16, 128),
            full(32, 24, 128),
            full(5, 8, width),
            full(5, 8, width),
            dma((14,)),
            dma((7,)),
            dma((7,)),
            dma((10, 4)),
            dma((10, 4)),
            dma((2, 4)),
            dma((2, 2, 4)),
            dma((2, 2, 4)),
            dma((3, 3, 4)),
            dma((3, 3, 4)),
            dma((5,)),
            dma((5,)),
            dma((5,)),
            dma((5,)),
        ]
        + reducing,
        compiler_params=params(collective_id=0, has_side_effects=True),
        name="layer",
    )(tokens, cot, wq, wo, wu, wd, gain, segments, cosine, sine, embedding, ada, bias)


def finish_kernel(
    up_ref, down_ref, left_ref, right_ref, qkv_ref, mixed_ref, dtok_ref, dada_ref, dbias_ref, dgain_ref,
    up_out, down_out, out_out, qkv_out, mixed_out, dtok_out, dada_out, dbias_out, dgain_out,
):
    dbias_out[...] = dbias_ref[0, :]
    dgain_out[...] = dgain_ref[0, :]
    up_out[...] = up_ref[...].astype(f32)
    down_out[...] = down_ref[...].astype(f32)
    out_out[...] = jnp.concatenate([left_ref[...], right_ref[...]], axis=1).astype(f32)
    qkv_out[...] = qkv_ref[...].astype(f32)
    mixed_out[...] = mixed_ref[...]
    dtok_out[...] = dtok_ref[...]
    dada_out[...] = jnp.concatenate([dada_ref[i] for i in range(3)], axis=1)


def finish_call(up, down, out, qkv, mixed, dtok, dada, dbias, dgain):
    steps = 8
    shape = jax.ShapeDtypeStruct
    halves, half = out.shape[0] // 2, out.shape[1]

    def rows(a):
        return pl.BlockSpec((a.shape[0] // steps, a.shape[1]), lambda i: (i, 0))

    def middle(a):
        return pl.BlockSpec((a.shape[0], a.shape[1] // steps, a.shape[2]), lambda i: (0, i, 0))

    part = (halves // steps, half)
    outs = [
        shape(up.shape, f32),
        shape(down.shape, f32),
        shape((halves, 2 * half), f32),
        shape(qkv.shape, f32),
        shape(mixed.shape, bf16),
        shape(dtok.shape, bf16),
        shape((dada.shape[1], 3 * dada.shape[2]), f32),
        shape(dbias.shape[1:], f32),
        shape(dgain.shape[1:], f32),
    ]

    def placed(a):
        if len(a.shape) == 1:
            return pl.BlockSpec(a.shape, lambda i: (0,))
        return rows(a) if len(a.shape) == 2 else middle(a)

    def whole(a):
        return pl.BlockSpec(a.shape, lambda i: (0, 0))

    return pl.pallas_call(
        finish_kernel,
        grid=(steps,),
        in_specs=[
            rows(up),
            rows(down),
            pl.BlockSpec(part, lambda i: (i, 0)),
            pl.BlockSpec(part, lambda i: (i + steps, 0)),
            middle(qkv),
            middle(mixed),
            middle(dtok),
            middle(dada),
            whole(dbias),
            whole(dgain),
        ],
        out_specs=[placed(o) for o in outs],
        out_shape=outs,
        compiler_params=params(),
        name="finish",
    )(up, down, out, out, qkv, mixed, dtok, dada, dbias, dgain)


def time_embedding(timestep):
    half = TEMB // 2
    frequency = jnp.exp(-math.log(10000.0) * jnp.arange(half, dtype=f32) / half)
    angles = timestep.astype(f32)[:, None] * frequency[None, :]
    return jnp.concatenate([jnp.cos(angles), jnp.sin(angles)], axis=-1)


def per_device(
    groups, tokens, segment_ids, timestep, ln_gain, w_qkv, w_out, w_up, w_down, ada_weight, ada_bias, cotangent
):
    half, width = tokens.shape[1], tokens.shape[2]
    length = 2 * half
    cosine, sine = (jnp.asarray(a) for a in rotary_np(length))
    embedding = time_embedding(timestep)

    _, _, _, _, d_up, d_down, d_out, d_qkv, mixed, dtok, d_ada_weight, d_ada_bias, dgain = layer_call(
        tokens, cotangent, w_qkv, w_out, w_up, w_down, ln_gain, segment_ids, cosine, sine,
        embedding, ada_weight, ada_bias,
    )
    d_up, d_down, d_out, d_qkv, mixed, dtok, d_ada_weight, d_ada_bias, d_gain = finish_call(
        d_up, d_down.reshape(-1, width), d_out, d_qkv, mixed, dtok, d_ada_weight.reshape(3, TEMB, width),
        d_ada_bias, dgain,
    )

    def rest(a):
        bit = 16
        while bit < groups:
            a = a + lax.ppermute(a, "dp", [(i, i ^ bit) for i in range(groups)])
            bit *= 2
        return a

    return (
        mixed,
        dtok,
        rest(d_gain),
        rest(d_qkv),
        rest(d_out),
        rest(d_up),
        rest(d_down),
        rest(d_ada_weight),
        rest(d_ada_bias),
    )


def solution(mesh):
    in_specs = (
        P("dp", "tensor", None),
        P("dp", None),
        P("dp"),
        P(),
        P(None, None, "tensor"),
        P("tensor", None),
        P(None, "tensor"),
        P("tensor", None),
        P(),
        P(),
        P("dp", "tensor", None),
    )
    out_specs = (
        P("dp", "tensor", None),
        P("dp", "tensor", None),
        P(),
        P(None, None, "tensor"),
        P("tensor", None),
        P(None, "tensor"),
        P("tensor", None),
        P(),
        P(),
    )
    return jax.shard_map(
        functools.partial(per_device, mesh.shape["dp"]), mesh=mesh, in_specs=in_specs, out_specs=out_specs, check_vma=False
    )
```

profile of v0, /device:TPU:0, one launch (start us, length us, event | category | flops | bytes accessed | tf_op | source)
XLA Modules:
  0.0 221.3 jit_solution(10727091898258381182)
XLA Ops:
  0.6 0.7 convert_element_type.3
  1.3 0.1 multiply_cosine_fusion
  1.4 0.6 pad_maximum_fusion.emb_ref
  2.1 207.3 %layer.1 = (bf16[3,768,384]{2,1,0:T(8,128)(2,1)}, bf16[384,768]{1,0:T(8,128)(2,1)}, bf16[768,1536]{1,0:T(8,128)(2,1)}, bf16[1536,768]{1,0:T(8,128)(2,1)}, bf16[7...) custom-call(bf16[2,512,768]{2,1,0:T(8,128)(2,1)} %tok.1, ...), custom_call_target="tpu_custom_call" | custom-call | tf_op jit(solution)/shard_map/layer/pallas_call | solution.py:1006
  209.4 11.7 %finish.1 = (f32[768,1536]{1,0:T(8,128)}, f32[1536,768]{1,0:T(8,128)}, f32[384,768]{1,0:T(8,128)}, f32[3,768,384]{2,1,0:T(8,128)}, bf16[2,512,768]{2,1,0:T(8,128...) custom-call(bf16[768,1536]{1,0:T(8,128)(2,1)} %get-tuple-element.27.up_ref, ...), custom_call_target="tpu_custom_call" | custom-call | tf_op jit(solution)/shard_map/finish/pallas_call | solution.py:1126
  (1 shorter events, 0.0 us)
where the time goes:
time: 222 us; the launch traced here: 221 us
  Pallas kernels  219 us (99%)
    pallas_call x1, Pallas kernels, layer_call(): pl.pallas_call(layer_kernel, in_specs=[any_] * 6 + [vm] * 7, out_specs=[a...  207 us
    pallas_call x1, Pallas kernels, finish_call(): pl.pallas_call(finish_kernel, grid=(steps,), in_specs=[rows(up), rows(dow...  11.7 us

commit v1 on v0

--- a/solution.py
+++ b/solution.py
@@ -837,7 +837,7 @@
         for stage, t in enumerate(times):
             at(t, move_event, stage, c)
     at(19, start_ffn, 0)
-    for stage, t in enumerate((22, 25, 27, 28)):
+    for stage, t in enumerate((22, 25, 28)):
         at(t, gather_event, ffn[0], stage)
     at(23, start_ffn, 1)
     for stage, t in enumerate((26, 28)):
@@ -917,23 +917,20 @@
         ).astype(bf16)
 
     gains[0] = jnp.zeros(gains.shape[1:], f32)
+    move_event(0, 3)
     move_event(2, 2)
-    gather_event(outs, 2)
-    move_event(0, 3)
 
     def after_rows(i):
         if i == 0:
-            move_event(3, 2)
             gather_event(gathers[1], 0)
-            gather_event(ffn[1], 2)
+            gather_event(ffn[0], 3)
         elif i == 1:
-            gather_event(outs, 3)
             move_event(1, 3)
             send_dtok.start()
-            move_event(4, 2)
-            start_qkv(2)
-            gather_event(ffn[1], 3)
+            move_event(3, 2)
+            gather_event(outs, 2)
         elif i == 2:
+            gather_event(ffn[1], 2)
             gather_event(gathers[1], 1)
 
     def last_step(i, carry):
@@ -948,7 +945,9 @@
 
     lax.fori_loop(0, blocks, last_step, 0)
     move_event(2, 3)
-    gather_event(gathers[2], 0)
+    move_event(4, 2)
+    start_qkv(2)
+    gather_event(outs, 3)
     gain_copy(0).start()
     keep_dtok = copy_here(modul.at[own_rows, :], dtok_out.at[side], 5)
     gather_event(gathers[1], 2)
@@ -965,17 +964,19 @@
     put_dada = copy_here(branch.at[pl.ds(0, 3 * TEMB), :], dada_out, 6)
     move_event(3, 3)
     gain_event(0)
-    gather_event(gathers[2], 1)
+    gather_event(ffn[1], 3)
     gather_event(gathers[1], 3)
+    gather_event(gathers[2], 0)
     move_event(4, 3)
     start_qkv(3)
     gain_event(1)
-    gather_event(gathers[2], 2)
+    gather_event(gathers[2], 1)
     gather_event(gathers[3], 0)
     gain_event(2)
-    gather_event(gathers[2], 3)
+    gather_event(gathers[2], 2)
     gather_event(gathers[3], 1)
     gain_event(3)
+    gather_event(gathers[2], 3)
     gather_event(gathers[3], 2)
     gather_event(gathers[3], 3)
     gain_event(4)
@@ -1092,7 +1093,7 @@
 
 
 def finish_call(up, down, out, qkv, mixed, dtok, dada, dbias, dgain):
-    steps = 8
+    steps = 4
     shape = jax.ShapeDtypeStruct
     halves, half = out.shape[0] // 2, out.shape[1]
 

time: 222 us -> 218 us (0.982)
  Pallas kernels: 219 us -> 215 us
    pallas_call x1, Pallas kernels: 207 us -> 204 us  [layer_call(): pl.pallas_call(layer_kernel, in_specs=[any_] * 6 + [vm] * 7, out_specs=[a...]
where the time goes in v1:
time: 218 us
  Pallas kernels  215 us (99%)
    pallas_call x1, Pallas kernels, layer_call(): pl.pallas_call(layer_kernel, in_specs=[any_] * 6 + [vm] * 7, out_specs=[a...  204 us
    pallas_call x1, Pallas kernels, finish_call(): pl.pallas_call(finish_kernel, grid=(steps,), in_specs=[rows(up), rows(dow...  11.3 us

profile of v1, /device:TPU:0, one launch (start us, length us, event | category | flops | bytes accessed | tf_op | source)
XLA Modules:
  0.0 217.7 jit_solution(3895755639725796309)
XLA Ops:
  0.6 0.7 convert_element_type.3
  1.3 0.1 multiply_cosine_fusion
  1.4 0.6 pad_maximum_fusion.emb_ref
  2.1 204.2 %layer.1 = (bf16[3,768,384]{2,1,0:T(8,128)(2,1)}, bf16[384,768]{1,0:T(8,128)(2,1)}, bf16[768,1536]{1,0:T(8,128)(2,1)}, bf16[1536,768]{1,0:T(8,128)(2,1)}, bf16[7...) custom-call(bf16[2,512,768]{2,1,0:T(8,128)(2,1)} %tok.1, ...), custom_call_target="tpu_custom_call" | custom-call | tf_op jit(solution)/shard_map/layer/pallas_call | solution.py:1007
  206.2 11.3 %finish.1 = (f32[768,1536]{1,0:T(8,128)}, f32[1536,768]{1,0:T(8,128)}, f32[384,768]{1,0:T(8,128)}, f32[3,768,384]{2,1,0:T(8,128)}, bf16[2,512,768]{2,1,0:T(8,128...) custom-call(bf16[768,1536]{1,0:T(8,128)(2,1)} %get-tuple-element.27.up_ref, ...), custom_call_target="tpu_custom_call" | custom-call | tf_op jit(solution)/shard_map/finish/pallas_call | solution.py:1127
  (1 shorter events, 0.0 us)

commit v2 on v1

--- a/solution.py
+++ b/solution.py
@@ -840,8 +840,7 @@
     for stage, t in enumerate((22, 25, 28)):
         at(t, gather_event, ffn[0], stage)
     at(23, start_ffn, 1)
-    for stage, t in enumerate((26, 28)):
-        at(t, gather_event, ffn[1], stage)
+    at(26, gather_event, ffn[1], 0)
     at(24, start_out)
     for stage, t in enumerate((26, 28)):
         at(t, gather_event, outs, stage)
@@ -924,13 +923,13 @@
         if i == 0:
             gather_event(gathers[1], 0)
             gather_event(ffn[0], 3)
+            gather_event(ffn[1], 1)
         elif i == 1:
             move_event(1, 3)
             send_dtok.start()
             move_event(3, 2)
             gather_event(outs, 2)
         elif i == 2:
-            gather_event(ffn[1], 2)
             gather_event(gathers[1], 1)
 
     def last_step(i, carry):
@@ -964,12 +963,13 @@
     put_dada = copy_here(branch.at[pl.ds(0, 3 * TEMB), :], dada_out, 6)
     move_event(3, 3)
     gain_event(0)
-    gather_event(ffn[1], 3)
+    gather_event(ffn[1], 2)
     gather_event(gathers[1], 3)
     gather_event(gathers[2], 0)
     move_event(4, 3)
     start_qkv(3)
     gain_event(1)
+    gather_event(ffn[1], 3)
     gather_event(gathers[2], 1)
     gather_event(gathers[3], 0)
     gain_event(2)

time: 218 us -> 222 us (1.018)
  Pallas kernels: 215 us -> 219 us
    pallas_call x1, Pallas kernels: 204 us -> 208 us  [layer_call(): pl.pallas_call(layer_kernel, in_specs=[any_] * 6 + [vm] * 7, out_specs=[a...]
where the time goes in v2:
time: 222 us; the launch traced here: 221 us
  Pallas kernels  219 us (99%)
    pallas_call x1, Pallas kernels, layer_call(): pl.pallas_call(layer_kernel, in_specs=[any_] * 6 + [vm] * 7, out_specs=[a...  208 us
    pallas_call x1, Pallas kernels, finish_call(): pl.pallas_call(finish_kernel, grid=(steps,), in_specs=[rows(up), rows(dow...  11.3 us

profile of v2, /device:TPU:0, one launch (start us, length us, event | category | flops | bytes accessed | tf_op | source)
XLA Modules:
  0.0 221.3 jit_solution(3207904378180437900)
XLA Ops:
  0.6 0.7 convert_element_type.3
  1.3 0.1 multiply_cosine_fusion
  1.4 0.6 pad_maximum_fusion.emb_ref
  2.1 207.8 %layer.1 = (bf16[3,768,384]{2,1,0:T(8,128)(2,1)}, bf16[384,768]{1,0:T(8,128)(2,1)}, bf16[768,1536]{1,0:T(8,128)(2,1)}, bf16[1536,768]{1,0:T(8,128)(2,1)}, bf16[7...) custom-call(bf16[2,512,768]{2,1,0:T(8,128)(2,1)} %tok.1, ...), custom_call_target="tpu_custom_call" | custom-call | tf_op jit(solution)/shard_map/layer/pallas_call | solution.py:1007
  209.8 11.3 %finish.1 = (f32[768,1536]{1,0:T(8,128)}, f32[1536,768]{1,0:T(8,128)}, f32[384,768]{1,0:T(8,128)}, f32[3,768,384]{2,1,0:T(8,128)}, bf16[2,512,768]{2,1,0:T(8,128...) custom-call(bf16[768,1536]{1,0:T(8,128)(2,1)} %get-tuple-element.27.up_ref, ...), custom_call_target="tpu_custom_call" | custom-call | tf_op jit(solution)/shard_map/finish/pallas_call | solution.py:1127
  (1 shorter events, 0.0 us)
